TPU v7x, 128 devices: a whole 4x4x4 slice. The times are simulated.
128 devices in a mesh: pipe: 4 (over x), dp: 32 (over z, y, core).
Axes of the slice: x: 4, y: 4, z: 4, core: 2. Of those that a mesh axis runs over, the one named last changes fastest.
Arguments:
- tokens: bfloat16 [4096, 1024], P('dp'), may hold values from -6 to 6
- cotangent: bfloat16 [4096, 1024], P('dp'), may hold values from -6 to 6
- live_counts: int32 [64], P('dp'), may hold values from 32 to 64, as said below
- segments: int32 [4096], P('dp'), may hold values from 0 to 255, never falling along the last dimension, each value on 1 to 64 neighbouring positions
- attn_input: bfloat16 [4, 1024, 3072], P('pipe', None, 'dp'), may hold values from -0.1875 to 0.1875
- attn_output: bfloat16 [4, 1024, 1024], P('pipe', None, 'dp'), may hold values from -0.1875 to 0.1875
- feed_up: bfloat16 [4, 1024, 4096], P('pipe', None, 'dp'), may hold values from -0.1875 to 0.1875
- feed_down: bfloat16 [4, 4096, 1024], P('pipe', None, 'dp'), may hold values from -0.09375 to 0.09375
- norm_gains: bfloat16 [4, 3, 1024], P('pipe', None, 'dp'), may hold values from 0.5 to 1.5
- vector_bias: bfloat16 [4, 7, 1024], P('pipe', None, 'dp'), may hold values from -2 to 2
- mid_gain: bfloat16 [4, 4096], P('pipe', 'dp'), may hold values from 0.5 to 1.5
- mid_bias: bfloat16 [4, 2, 4096], P('pipe', None, 'dp'), may hold values from -2 to 2
- head_scale: bfloat16 [4, 16], P('pipe'), may hold values from 0.25 to 1.75
Outputs:
- section_outputs: bfloat16 [4, 4096, 1024], P('pipe', 'dp')
- input_grads: bfloat16 [4, 4096, 1024], P('pipe', 'dp')
- grad_attn_input: float32 [4, 1024, 3072], P('pipe', None, 'dp')
- grad_attn_output: float32 [4, 1024, 1024], P('pipe', None, 'dp')
- grad_feed_up: float32 [4, 1024, 4096], P('pipe', None, 'dp')
- grad_feed_down: float32 [4, 4096, 1024], P('pipe', None, 'dp')
- grad_norm_gains: float32 [4, 3, 1024], P('pipe', None, 'dp')
- grad_vector_bias: float32 [4, 7, 1024], P('pipe', None, 'dp')
- grad_mid_gain: float32 [4, 4096], P('pipe', 'dp')
- grad_mid_bias: float32 [4, 2, 4096], P('pipe', None, 'dp')
- grad_head_scale: float32 [4, 16], P('pipe')
Inputs may be any that keep to these rules, and one draw needn't show every extreme that they name: `live_counts`: some pack holds 64 live tokens.
All inputs are finite; a program needn't handle non-finite values.
Results may differ from a plain program's by a relative error of at most 0.035.
Values may be sent and summed in bfloat16 or wider, within the bound.
A program may use at most 960 MiB of HBM per device.

v0:
```python
import jax
import jax.numpy as jnp
from jax import lax
from jax.experimental import pallas as pl
from jax.experimental.pallas import tpu as pltpu
from jax.sharding import PartitionSpec as P

MESH = pl.DeviceIdType.MESH
EPS = 1e-05
F32, BF16 = jnp.float32, jnp.bfloat16
VMEM_LIMIT = 61840 * 1024

TOK, WIDTH, FF, QKV = 128, 1024, 4096, 3072
IN, OUT, UP, DOWN, UNITS = 0, 6, 8, 16, 24
SMALL = "small"
GATHER = (SMALL, (IN, 6), (OUT, 2), (UP, 8), (DOWN + 4, 4), (DOWN, 4))
SCATTER_STEPS = ((0,), (1,), (2,), (3,), (4, 5), (6,))
SCATTER = ((DOWN + 4, 4), (UP, 4), (UP + 4, 4), (IN, 4), SMALL, (IN + 4, 4), (DOWN, 4))
LENT = (DOWN, 4)
LATE, HELP = 5, 6
AWAY, AID = 6, 7
DESK = (DOWN + 4, 4)
X_OWN, X_GIVE, X_SUMS, X_BACK = 0, 1, 5, 8
BACK_GROUPS = (
    ((1, 0), (2, 0), (3, 0)),
    ((0, 1), (0, 2), (1, 1), (1, 2)),
    ((2, 1), (2, 2), (3, 1), (3, 2)),
    ((0, 3), (1, 3), (2, 3), (3, 3)),
)
SHARE = 3
OFFS = (0, 3, 1, 2)


class Place:
    def __init__(self):
        self.s = lax.axis_index("pipe")
        d = lax.axis_index("dp")
        self.d = d
        self.c = d % 2
        y, z = (d // 2) % 4, d // 8
        self.f = y + self.c * (z - y)
        self.g = z + self.c * (y - z)
        self.sf = 2 + 6 * self.c
        self.sg = 8 - 6 * self.c
        self.sib = d + 1 - 2 * self.c
        rows = [((self.f + i) % 4) * self.sf for i in range(4)]
        columns = [((self.g + i) % 4) * self.sg for i in range(4)]
        self.table = [[row + column + self.c for column in columns] for row in rows]
        self.flip = 1 - 2 * self.c

    def dp(self, of, og):
        return self.table[of % 4][og % 4]

    def sib_dp(self, of, og):
        return self.table[og % 4][of % 4] + self.flip

    def greet(self):
        sem = pltpu.get_barrier_semaphore()
        near = [self.dp(1, 0), self.dp(3, 0), self.dp(0, 1), self.dp(0, 3), self.sib]
        near = [(self.s, to) for to in near] + [((self.s + by) % 4, self.d) for by in (1, 3)]
        for to in near:
            pl.semaphore_signal(sem, inc=1, device_id=to, device_id_type=MESH)

    def barrier(self):
        pl.semaphore_wait(pltpu.get_barrier_semaphore(), 7)


class Work:
    def __init__(self):
        self.items = []

    def add(self, slice_of_work, when=None, tag=None):
        self.items.append((slice_of_work, when, tag))

    def pop(self, count=1):
        for _ in range(min(count, len(self.items))):
            slice_of_work, when, _ = self.items.pop(0)
            if when is None:
                slice_of_work()
            else:
                pl.when(when)(slice_of_work)

    def until(self, tag):
        while any(tag == item[2] for item in self.items):
            self.pop()

    def drain(self):
        self.pop(len(self.items))


def remote(src, dst, send, recv, s, to):
    return pltpu.make_async_remote_copy(
        src_ref=src, dst_ref=dst, send_sem=send, recv_sem=recv, device_id=(s, to), device_id_type=MESH
    )


def piece_block(whole, small, piece, d, half=None):
    if piece is SMALL:
        return small.at[d] if half is None else small.at[d, pl.ds(8 * half, 8)]
    u, n = piece
    return whole.at[d, pl.ds(u, n)] if half is None else whole.at[d, pl.ds(u + half * (n // 2), n // 2)]


def blocks(whole, small, piece, count, first=0):
    if piece is SMALL:
        return small.at[pl.ds(first, count)]
    return whole.at[pl.ds(first, count), pl.ds(*piece)]


class Gather:
    def __init__(self, place, whole, small, lent, send, recv, xsend, xrecv):
        self.p, self.whole_ref, self.small, self.lent = place, whole, small, lent
        self.send, self.recv, self.xsend, self.xrecv = send, recv, xsend, xrecv
        self.work = Work()

    def ref(self, k, d, half=None):
        if k == HELP:
            u, n = LENT
            at = pl.ds(u, n) if half is None else pl.ds(u + half * (n // 2), n // 2)
            return self.lent.at[d // 2, at]
        return piece_block(self.whole_ref, self.small, GATHER[k], d, half)

    def put(self, k, slot, d, half, to):
        ref = self.ref(k, d, half)
        remote(ref, ref, self.send.at[k], self.recv.at[k, slot], self.p.s, to).start()

    def got(self, k, slot, d):
        ref = self.ref(k, d)
        remote(ref, ref, self.send.at[k], self.recv.at[k, slot], self.p.s, self.p.sib).wait_recv()

    def hand(self, k, j, i):
        p = self.p
        d = p.dp(OFFS[j], OFFS[i])
        if k != HELP:
            self.put(k, 15, d, None, p.sib)
        elif (j, i) != (0, 0):
            self.give(j, i).start()

    def give(self, j, i):
        p = self.p
        d = p.dp(OFFS[j], OFFS[i])
        group = next(g for g, group in enumerate(BACK_GROUPS) if (j, i) in group)
        return remote(
            self.ref(HELP, d), self.ref(LATE, d), self.xsend.at[1], self.xrecv.at[X_GIVE + group], (p.s + 1) % 4, p.d
        )

    def lend(self):
        p = self.p
        return remote(
            self.ref(LATE, p.d), self.ref(HELP, p.d), self.xsend.at[0], self.xrecv.at[X_OWN], (p.s + 3) % 4, p.d
        )

    def spread(self, k, j):
        p = self.p
        d = p.dp(OFFS[j], 0)
        self.put(k, 3 + 3 * j, d, None, p.dp(0, 1))
        self.put(k, 4 + 3 * j, d, None, p.dp(0, 3))
        self.hand(k, j, 0)

    def first(self, k):
        p = self.p
        self.put(k, 0, p.d, None, p.dp(1, 0))
        self.put(k, 1, p.d, None, p.dp(3, 0))
        self.spread(k, 0)

    def ring(self, k):
        p = self.p
        left, right = p.dp(3, 0), p.dp(1, 0)
        self.got(k, 0, left)
        self.put(k, 2, left, 0, right)
        self.spread(k, 1)
        self.got(k, 1, right)
        self.put(k, 2, right, 1, left)
        self.spread(k, 2)

    def far(self, k):
        self.got(k, 2, self.p.dp(2, 0))
        self.spread(k, 3)

    def second(self, k, j):
        p = self.p
        low, high = p.dp(OFFS[j], 3), p.dp(OFFS[j], 1)
        self.got(k, 3 + 3 * j, low)
        self.put(k, 5 + 3 * j, low, 0, p.dp(0, 1))
        self.hand(k, j, 1)
        self.got(k, 4 + 3 * j, high)
        self.put(k, 5 + 3 * j, high, 1, p.dp(0, 3))
        self.hand(k, j, 2)

    def last(self, k, j):
        self.got(k, 5 + 3 * j, self.p.dp(OFFS[j], 2))
        self.hand(k, j, 3)

    def relay(self, group):
        p = self.p
        ref = self.many(LATE, len(BACK_GROUPS[group]))
        remote(ref, ref, self.xsend.at[1], self.xrecv.at[X_GIVE + group], p.s, p.sib).wait_recv()
        for j, i in BACK_GROUPS[group]:
            self.hand(LATE, j, i)

    def many(self, k, count):
        if k == HELP:
            return blocks(self.lent, None, LENT, count)
        return blocks(self.whole_ref, self.small, GATHER[k], count)

    def whole(self, k):
        ref = self.many(k, 16)
        remote(ref, ref, self.send.at[k], self.recv.at[k, 15], self.p.s, self.p.sib).wait_recv()

    def close(self):
        p = self.p

        def sent(k, count):
            ref = self.many(k, count)
            remote(ref, ref, self.send.at[k], self.recv.at[k, 15], p.s, p.sib).wait_send()

        for k in range(len(GATHER)):
            if k != LATE:
                sent(k, 31)

        @pl.when(p.s > 0)
        def _():
            sent(LATE, 31)

        @pl.when(p.s == 0)
        def _():
            sent(LATE, 16)
            self.lend().wait_send()

        @pl.when(p.s == 3)
        def _():
            sent(HELP, 15)
            ref = self.many(HELP, 15)
            remote(ref, ref, self.xsend.at[1], self.xrecv.at[X_GIVE], p.s, p.sib).wait_send()

    def run(self, own, ready):
        n, begun = len(GATHER), 0
        s = self.p.s

        def stage(step, k):
            if k == LATE:
                pl.when(s > 0)(lambda: step(k))
            elif 0 <= k < n:
                step(k)

        own(LATE)

        @pl.when(s == 0)
        def _():
            self.lend().start()
            self.hand(LATE, 0, 0)

        @pl.when(s == 3)
        def _():
            self.lend().wait_recv()
            for step in (self.first, self.ring, self.far):
                step(HELP)
            for j in range(4):
                self.second(HELP, j)
            for j in range(4):
                self.last(HELP, j)

        for t in range(n + 3):
            while begun < min(n, t + 3):
                if begun != LATE:
                    own(begun)
                stage(self.first, begun)
                begun += 1
            stage(self.ring, t)
            self.work.pop()
            stage(self.far, t - 1)
            self.work.pop()
            for j in range(4):
                stage(lambda k, j=j: self.second(k, j), t - 2)
                self.work.pop()
            for j in range(4):
                stage(lambda k, j=j: self.last(k, j), t - 3)
                self.work.pop()
            if 4 <= t < 8:
                pl.when(s == 0)(lambda t=t: self.relay(t - 4))

            self.work.pop()
            if t >= 3:
                self.whole(t - 3)
                ready(t - 3)
        self.work.drain()


def dot(a, b, ca, cb):
    return lax.dot_general(a, b, (((ca,), (cb,)), ((), ())), preferred_element_type=F32)


def centered(x):
    c = x - jnp.mean(x, axis=-1, keepdims=True)
    r = lax.rsqrt(jnp.mean(c * c, axis=-1, keepdims=True) + EPS)
    return c, r


def norm(x, gain, bias):
    c, r = centered(x)
    return c * r * gain + bias


def norm_back(x, gain, gy):
    c, r = centered(x)
    hat = c * r
    gh = gy * gain
    gx = r * (gh - jnp.mean(gh, axis=-1, keepdims=True) - hat * jnp.mean(gh * hat, axis=-1, keepdims=True))
    return gx, gy * hat


def rows_of(i, n):
    return pl.ds(pl.multiple_of(i * n, n), n)


def col_sum(x):
    return jnp.sum(x, axis=0, keepdims=True)


def row_sum(x):
    return dot(jnp.full((16, x.shape[0]), 1.0, BF16), x, 1, 0)[:1]


K0, K1 = 0.7978845608028654, 0.044715


def gelu(x):
    return 0.5 * x * (1.0 + jnp.tanh(K0 * (x + K1 * x * x * x)))


def gelu_both(x):
    t = jnp.tanh(K0 * (x + K1 * x * x * x))
    u = 0.5 * x * (1.0 + t)
    du = 0.5 * (1.0 + t) + 0.5 * x * (1.0 - t * t) * K0 * (1.0 + 3.0 * K1 * x * x)
    return u, du


def head_masks():
    lane = lax.broadcasted_iota(jnp.int32, (1, 128), 1)
    even = jnp.where(lane < 64, 1.0, 0.0)
    return even.astype(BF16), (1.0 - even).astype(BF16)


def two_rows(x, even, odd):
    return jnp.concatenate([x * even, x * odd], axis=0)


def each(count, unroll=1):
    def run(body):
        def step(i, carry):
            body(i)
            return carry

        lax.fori_loop(0, count, step, 0, unroll=unroll)

    return run


def stack(w, d0, nd, u, nu, cols=slice(0, WIDTH)):
    return w[pl.ds(d0, nd), u : u + nu, :, cols].reshape(nd * nu * 16, cols.stop - cols.start)


def head_columns():
    col = lax.broadcasted_iota(jnp.int32, (128, WIDTH), 1)
    head = lax.broadcasted_iota(jnp.int32, (128, WIDTH), 0)
    return jnp.where(col // 64 == head, 1.0, 0.0)


class Layer:
    def __init__(self, w, r):
        self.w, self.r = w, r


    def first_norm(self):
        r, pd = self.r, self.r["pd"]

        @each(4, 2)
        def _(i):
            at = rows_of(i, 32)
            r["a1"][at, :] = norm(r["zin"][at, :].astype(F32), pd[0:1, :], pd[3:4, :]).astype(BF16)

    def qkv(self, first=0, count=4):
        r = self.r

        @each(count, 4 if count == 4 else 1)
        def _(c):
            c = c + first
            at = rows_of(c, 768)
            acc = dot(r["a1"][...], stack(self.w, 8 * c, 8, IN, 6), 1, 1) + r["pq"][0:1, at]
            r["qkv"][:, at] = acc.astype(BF16)

    def attention(self, first=0, count=8):
        r, qkv = self.r, self.r["qkv"]
        even, odd = head_masks()

        @each(count, 4 if count == 8 else 1)
        def _(p):
            p = p + first
            cols = rows_of(p, 128)
            q = qkv[:, cols]
            k = qkv[:, pl.ds(pl.multiple_of(WIDTH + p * 128, 128), 128)]
            v = qkv[:, pl.ds(pl.multiple_of(2 * WIDTH + p * 128, 128), 128)]
            ok = r["ok"][...]
            sc = dot(two_rows(q, even, odd), k, 1, 1) * 0.125
            sc = jnp.where(jnp.concatenate([ok, ok], axis=0) > 0.5, sc, -1000000000.0)
            e = jnp.exp(sc - jnp.max(sc, axis=-1, keepdims=True))
            pr = e / jnp.sum(e, axis=-1, keepdims=True)
            r["p"][rows_of(p, 256), :] = pr
            pb = pr.astype(BF16)
            both = jnp.concatenate([pb[:TOK], pb[TOK:]], axis=1)
            mixed = dot(both, two_rows(v, even, odd), 1, 0)
            r["mixed"][:, cols] = mixed
            r["scaled"][:, cols] = (mixed * r["hs"][0:1, cols]).astype(BF16)

    def project(self):
        r = self.r
        r["attn"][...] = dot(r["scaled"][...], stack(self.w, 0, 32, OUT, 2), 1, 1) + r["pd"][6:7, :]

    def middle_norms(self):
        r, pd = self.r, self.r["pd"]

        @each(4, 2)
        def _(i):
            at = rows_of(i, 32)
            z2 = r["zin"][at, :].astype(F32) + norm(r["attn"][at, :], pd[1:2, :], pd[7:8, :])
            r["z2"][at, :] = z2
            r["a2"][at, :] = norm(z2, pd[2:3, :], pd[8:9, :]).astype(BF16)

    def up(self, first=0, count=4):
        r = self.r

        @each(count)
        def _(c):
            c = c + first
            cols = rows_of(c, 1024)
            r["ff"][:, cols] = dot(r["a2"][...], stack(self.w, 8 * c, 8, UP, 8), 1, 1) + r["pm"][11:12, cols]

    def inner_norm(self, first=0, count=8):
        r, pm = self.r, self.r["pm"]

        @each(count, 2)
        def _(i):
            i = i + first
            at = rows_of(i, 16)
            r["mid"][at, :] = norm(gelu(r["ff"][at, :]), pm[10:11, :], pm[12:13, :]).astype(BF16)

    def down(self, send_out):
        r = self.r
        for n in range(4):
            cols = slice(n * 256, (n + 1) * 256)
            acc = r["z2"][:, cols] + r["pd"][9:10, cols]
            for q in range(4):
                w = stack(self.w, 8 * n, 8, DOWN + 2 * q, 2)
                acc = acc + dot(r["mid"][:, q * 1024 : (q + 1) * 1024], w, 1, 1)
            r["out"][:, cols] = acc.astype(BF16)
            send_out(n)

    def prepare(self):
        r = self.r

        @each(8, 2)
        def _(i):
            at = rows_of(i, 16)
            u, du = gelu_both(r["ff"][at, :])
            c, s = centered(u)
            r["hat"][at, :] = (c * s).astype(BF16)
            r["slope"][at, :] = (du * s).astype(BF16)

        for name in ("gd", "gm"):
            r[name][...] = jnp.zeros_like(r[name])


    def back_down(self, *chunks):
        r = self.r
        for q in chunks:
            w = stack(self.w, 0, 32, DOWN + 2 * q, 2)
            r["ff"][:, q * 1024 : (q + 1) * 1024] = dot(r["gin"][...], w, 1, 0)

    def back_inner(self, first=0, count=8):
        r, pm = self.r, self.r["pm"]

        @each(count, 2)
        def _(i):
            i = i + first
            at = rows_of(i, 16)
            gh = r["ff"][at, :] * pm[10:11, :]
            hat = r["hat"][at, :].astype(F32)
            m1 = jnp.mean(gh, axis=-1, keepdims=True)
            m2 = jnp.mean(gh * hat, axis=-1, keepdims=True)
            r["ghid"][at, :] = ((gh - m1 - hat * m2) * r["slope"][at, :].astype(F32)).astype(BF16)

    def back_up(self, cols=slice(0, WIDTH)):
        r = self.r
        r["tw"][:, cols] = dot(r["ghid"][...], stack(self.w, 0, 32, UP, 8, cols), 1, 0)

    def back_middle(self):
        r, gd, pd = self.r, self.r["gd"], self.r["pd"]

        @each(4, 2)
        def _(i):
            at = rows_of(i, 32)
            ga2 = r["tw"][at, :]
            gz, gg = norm_back(r["z2"][at, :], pd[2:3, :], ga2)
            gd[2:3, :] += col_sum(gg)
            gd[8:9, :] += col_sum(ga2)
            gz = gz + r["gin"][at, :].astype(F32)
            r["gz2"][at, :] = gz
            gat, gg = norm_back(r["attn"][at, :], pd[1:2, :], gz)
            gd[1:2, :] += col_sum(gg)
            gd[7:8, :] += col_sum(gz)
            r["gattn"][at, :] = gat.astype(BF16)

    def back_project(self):
        r = self.r
        r["tw"][...] = dot(r["gattn"][...], stack(self.w, 0, 32, OUT, 2), 1, 0)

    def back_attention(self, first=0, count=8):
        r = self.r
        even, odd = head_masks()

        @each(count, 4 if count == 8 else 1)
        def _(p):
            p = p + first
            cols = rows_of(p, 128)
            kcols = pl.ds(pl.multiple_of(WIDTH + p * 128, 128), 128)
            vcols = pl.ds(pl.multiple_of(2 * WIDTH + p * 128, 128), 128)
            gs = r["tw"][:, cols]
            r["gh"][0:1, cols] = col_sum(gs * r["mixed"][:, cols])
            gmx = (gs * r["hs"][0:1, cols]).astype(BF16)
            q, k, v = r["qkv"][:, cols], r["qkv"][:, kcols], r["qkv"][:, vcols]
            gmx2 = two_rows(gmx, even, odd)
            gp = dot(gmx2, v, 1, 1)
            pr = r["p"][rows_of(p, 256), :]
            gsc = (pr * (gp - jnp.sum(pr * gp, axis=-1, keepdims=True))).astype(BF16)
            both = jnp.concatenate([gsc[:TOK], gsc[TOK:]], axis=1)
            r["gqkv"][:, cols] = (dot(both, two_rows(k, even, odd), 1, 0) * 0.125).astype(BF16)
            r["gqkv"][:, kcols] = (dot(gsc, two_rows(q, even, odd), 0, 0) * 0.125).astype(BF16)
            r["gqkv"][:, vcols] = dot(pr.astype(BF16), gmx2, 0, 0).astype(BF16)

    def back_qkv(self, cols=slice(0, WIDTH)):
        r = self.r
        r["tw"][:, cols] = dot(r["gqkv"][...], stack(self.w, 0, 32, IN, 6, cols), 1, 0)

    def back_first(self, send_out):
        r, gd, pd = self.r, self.r["gd"], self.r["pd"]
        for i in range(4):
            at = slice(i * 32, (i + 1) * 32)
            ga1 = r["tw"][at, :]
            gz, gg = norm_back(r["zin"][at, :].astype(F32), pd[0:1, :], ga1)
            r["gz"][at, :] = (gz + r["gz2"][at, :]).astype(BF16)
            send_out(i)
            gd[0:1, :] += col_sum(gg)
            gd[3:4, :] += col_sum(ga1)

    def inner_sums(self):
        r, gm = self.r, self.r["gm"]

        @each(8)
        def _(i):
            at = rows_of(i, 16)
            g = r["ff"][at, :]
            gm[10:11, :] += col_sum(g * r["hat"][at, :].astype(F32))
            gm[12:13, :] += col_sum(g)

        gm[11:12, :] = row_sum(r["ghid"][...])

    def other_sums(self):
        r, gd = self.r, self.r["gd"]
        gd[9:10, :] = row_sum(r["gin"][...])
        gd[6:7, :] = row_sum(r["gattn"][...])
        gd[4:5, :] = row_sum(r["gqkv"][:, :WIDTH])
        gd[5:6, :] = row_sum(r["gqkv"][:, 2 * WIDTH :])


    def grad_down(self, *chunks):
        r = self.r

        @each(4)
        def _(c):
            gt = r["gin"][:, rows_of(c, 256)].T
            for q in chunks:
                g = dot(gt, r["mid"][:, q * 1024 : (q + 1) * 1024], 1, 0).astype(BF16)
                self.w[pl.ds(8 * c, 8), DOWN + 2 * q : DOWN + 2 * q + 2] = g.reshape(8, 2, 16, WIDTH)

    def grad_up(self, first, count):
        r = self.r

        @each(count)
        def _(c):
            c = c + first
            g = dot(r["ghid"][:, rows_of(c, 512)].T, r["a2"][...], 1, 0).astype(BF16)
            self.w[pl.ds(4 * c, 4), UP : UP + 8] = g.reshape(4, 8, 16, WIDTH)

    def grad_in(self, first, count):
        r = self.r

        @each(count)
        def _(c):
            c = c + first
            g = dot(r["gqkv"][:, rows_of(c, 384)].T, r["a1"][...], 1, 0).astype(BF16)
            self.w[pl.ds(4 * c, 4), IN : IN + 6] = g.reshape(4, 6, 16, WIDTH)

    def grad_out(self, c):
        r = self.r
        g = dot(r["gattn"][:, c * 512 : (c + 1) * 512].T, r["scaled"][...], 1, 0).astype(BF16)
        self.w[pl.ds(16 * c, 16), OUT : OUT + 2] = g.reshape(16, 2, 16, WIDTH)

    def grad_small(self, small):
        r = self.r
        hsum = lax.dot_general(
            jnp.broadcast_to(r["gh"][0:1, :], (8, WIDTH)), head_columns(), (((1,), (1,)), ((), ())),
            precision=lax.Precision.HIGHEST, preferred_element_type=F32,
        )
        is13 = lax.broadcasted_iota(jnp.int32, (16, 128), 0) == 13
        heads = jnp.where(is13, jnp.concatenate([hsum, hsum], axis=0), 0.0)
        for d in range(32):
            a, b = (d // 4) * 128, d * 128
            small[d] = r["gd"][:, a : a + 128] + r["gm"][:, b : b + 128] + heads


class Scatter:
    def __init__(self, place, grads, small, sib, ssib, land, sland, back, send, recv, xsend, xrecv):
        self.p, self.grads, self.small = place, grads, small
        self.sib, self.ssib, self.land, self.sland, self.back = sib, ssib, land, sland, back
        self.send, self.recv, self.xsend, self.xrecv = send, recv, xsend, xrecv
        self.work = Work()

    def copy(self, k, slot, src, dst, to):
        return remote(src, dst, self.send.at[k], self.recv.at[k, slot], self.p.s, to)

    def go(self, k, slot, src, dst, to):
        self.copy(k, slot, src, dst, to).start()

    def got(self, k, slot, dst):
        self.copy(k, slot, dst, dst, self.p.sib).wait_recv()

    def block(self, k, of, og, half=None):
        d = self.p.dp(of, og)
        if k == AID:
            return piece_block(self.sib, None, DESK, d // 2, half)
        return piece_block(self.grads, self.small, SCATTER[k], d, half)

    def from_sib(self, k, slot, half=None):
        return piece_block(self.sib, self.ssib, SCATTER[k], slot, half)

    def landing(self, k, kind, slot):
        if k != AID and SCATTER[k] is SMALL:
            return self.sland[kind].at[slot]
        step = next((t for t, ks in enumerate(SCATTER_STEPS) if k in ks), len(SCATTER_STEPS))
        return self.land[kind].at[step % SHARE, slot]

    def landed(self, k, slot, kind, j=0):
        self.got(k, slot, self.landing(k, kind, pl.ds(2 * j, 2)))

    def to_sibling(self, k):
        p = self.p
        for i in (3, 1, 2, 0):
            for j in (3, 1, 2, 0):
                src = piece_block(self.grads, self.small, SCATTER[k], p.sib_dp(OFFS[j], OFFS[i]))
                self.go(k, 0 if i == 3 else 1, src, self.from_sib(k, i * 4 + j), p.sib)

    def lent_sum(self, i, j):
        p = self.p
        return remote(
            self.block(AWAY, OFFS[j], OFFS[i]), self.block(AID, OFFS[j], OFFS[i]), self.xsend.at[2],
            self.xrecv.at[X_SUMS + (2, 1, 1, 0)[i]], (p.s + 3) % 4, p.d,
        )

    def lend(self):
        for i in (3, 1, 2, 0):
            if i in (3, 1):
                self.arrived(AWAY, i == 3)
            for j in (3, 1, 2, 0):
                self.add(AWAY, self.block(AWAY, OFFS[j], OFFS[i]), [self.from_sib(AWAY, i * 4 + j)])
                self.lent_sum(i, j).start()

    def returned(self):
        p = self.p
        return remote(
            self.block(AID, 0, 0), self.back, self.xsend.at[3], self.xrecv.at[X_BACK], (p.s + 1) % 4, p.d
        )

    def arrived(self, k, far):
        first, count = (12, 4) if far else (0, 12)
        self.got(k, 0 if far else 1, blocks(self.sib, self.ssib, SCATTER[k], count, first))

    def lent_arrived(self, group):
        ref = blocks(self.sib, None, DESK, (4, 8, 4)[group])
        remote(ref, ref, self.xsend.at[2], self.xrecv.at[X_SUMS + group], self.p.s, self.p.sib).wait_recv()

    def add(self, k, dst, srcs, store=None):
        out = dst if store is None else store
        if store is None and not srcs:
            return
        if k != AID and SCATTER[k] is SMALL:
            out[...] = dst[...] + sum(src[...] for src in srcs)
            return

        @each(dst.shape[0])
        def _(u):
            acc = dst[u].astype(F32)
            for src in srcs:
                acc = acc + src[u].astype(F32)
            out[u] = acc.astype(out.dtype)

    def halves(self, k, j):
        p = self.p
        srcs = []
        if k == AID:
            if j == 3:
                self.lent_arrived(0)
        else:
            if j == 3:
                self.arrived(k, True)
            srcs = [self.from_sib(k, 12 + j)]
        self.add(k, self.block(k, OFFS[j], 2), srcs)
        for side, to in enumerate((p.dp(0, 1), p.dp(0, 3))):
            self.go(k, 2 + j, self.block(k, OFFS[j], 2, side), self.landing(k, 0, 2 * j + side), to)

    def wholes(self, k, j):
        p = self.p
        if j == 3:
            if k == AID:
                self.lent_arrived(1)
            else:
                self.arrived(k, False)
        self.landed(k, 2 + j, 0, j)
        for i, near, side in ((2, 1, 0), (1, 3, 1)):
            for half in range(2):
                srcs = [] if k == AID else [self.from_sib(k, i * 4 + j, half)]
                if half == side:
                    srcs.append(self.landing(k, 0, 2 * j + side))
                self.add(k, self.block(k, OFFS[j], near, half), srcs)
        for near, side in ((1, 0), (3, 1)):
            self.go(k, 6 + j, self.block(k, OFFS[j], near), self.landing(k, 1, 2 * j + side), p.dp(0, near))

    def far(self, k, j):
        p = self.p
        srcs = []
        if k != AID:
            srcs.append(self.from_sib(k, j))
        elif j == 3:
            self.lent_arrived(2)
        self.landed(k, 6 + j, 1, j)
        srcs += [self.landing(k, 1, 2 * j + side) for side in range(2)]
        self.add(k, self.block(k, OFFS[j], 0), srcs)
        if j == 3:
            self.go(k, 10, self.block(k, 2, 0, 0), self.landing(k, 2, 0), p.dp(1, 0))
            self.go(k, 10, self.block(k, 2, 0, 1), self.landing(k, 2, 1), p.dp(3, 0))

    def near(self, k):
        p = self.p
        self.landed(k, 10, 2)
        for near, side in ((1, 0), (3, 1)):
            self.add(k, self.block(k, near, 0, side), [self.landing(k, 2, side)])
        for near, side in ((1, 0), (3, 1)):
            self.go(k, 11, self.block(k, near, 0), self.landing(k, 3, side), p.dp(near, 0))

    def last(self, k, total, small_total):
        self.landed(k, 11, 3)
        srcs = [self.landing(k, 3, side) for side in range(2)]
        if k == AID:
            self.add(k, self.block(k, 0, 0), srcs)
            self.returned().start()
        elif SCATTER[k] is SMALL:
            self.add(k, self.block(k, 0, 0), srcs, store=small_total)
        else:
            u, n = SCATTER[k]
            self.add(k, self.block(k, 0, 0), srcs, store=total.at[pl.ds(u, n)])

    def aid(self):
        for step in (self.halves, self.wholes, self.far):
            for j in (3, 1, 2, 0):
                step(AID, j)
        self.near(AID)
        self.last(AID, None, None)

    def close(self):
        p = self.p

        def sent(k, count):
            if k == AID:
                ref = blocks(self.sib, None, DESK, count)
            else:
                ref = blocks(self.grads, self.small, SCATTER[k], count)
            self.copy(k, 0, ref, ref, p.sib).wait_send()

        for k in range(len(SCATTER)):
            if k != AWAY:
                sent(k, 31)

        @pl.when(p.s > 0)
        def _():
            sent(AWAY, 31)

        @pl.when(p.s == 0)
        def _():
            sent(AWAY, 16)
            ref = blocks(self.grads, None, LENT, 16)
            remote(ref, ref, self.xsend.at[2], self.xrecv.at[X_SUMS], p.s, p.sib).wait_send()

        @pl.when(p.s == 3)
        def _():
            sent(AID, 15)
            self.returned().wait_send()


HELD = dict(
    pd=((16, WIDTH), F32), pm=((16, FF), F32), pq=((1, QKV), F32), hs=((8, WIDTH), F32), ok=((TOK, TOK), F32),
    zin=((TOK, WIDTH), BF16), a1=((TOK, WIDTH), BF16), qkv=((TOK, QKV), BF16), p=((8 * 256, TOK), F32),
    mixed=((TOK, WIDTH), F32), scaled=((TOK, WIDTH), BF16), attn=((TOK, WIDTH), F32), z2=((TOK, WIDTH), F32),
    a2=((TOK, WIDTH), BF16), ff=((TOK, FF), F32), hat=((TOK, FF), BF16), slope=((TOK, FF), BF16), mid=((TOK, FF), BF16),
    gin=((TOK, WIDTH), BF16), ghid=((TOK, FF), BF16), gattn=((TOK, WIDTH), BF16), gqkv=((TOK, QKV), BF16),
    tw=((TOK, WIDTH), F32), gz2=((TOK, WIDTH), F32), gd=((16, WIDTH), F32), gm=((16, FF), F32), gh=((8, WIDTH), F32),
)
LANDING = ((8, 2), (8, 4), (2, 2), (2, 4))


def kernel(*refs):
    (tok, cot, live, seg, own_in, own_out, own_up, own_down, gains, vecs, mgain, mbias, hscale), refs = refs[:13], refs[13:]
    (out, gz, total, small_total), refs = refs[:4], refs[4:]
    (w, small, sib, ssib), refs = refs[:4], refs[4:]
    land, sland, refs = refs[:4], refs[4:8], refs[8:]
    back, refs = refs[0], refs[1:]
    r = dict(zip(HELD, refs), out=out, gz=gz)
    gsend, grecv, own_sem, xsend, xrecv, bsend, brecv, ssend, srecv, hsend, hrecv, sib_ok, lent_ok = refs[len(HELD) :]
    place = Place()
    layer = Layer(w, r)
    place.greet()

    loads = [
        pltpu.make_async_copy(
            own_down.at[:, :, pl.ds(q * 1024, 1024)], w.at[place.d, pl.ds(DOWN + 2 * q, 2)], own_sem.at[q]
        )
        for q in range(4)
    ] + [
        pltpu.make_async_copy(own_in, w.at[place.d, pl.ds(IN, 6)], own_sem.at[4]),
        pltpu.make_async_copy(own_out, w.at[place.d, pl.ds(OUT, 2)], own_sem.at[5]),
    ]
    for copy in loads:
        copy.start()
    token_load = pltpu.make_async_copy(tok, r["zin"], own_sem.at[6])
    cot_load = pltpu.make_async_copy(cot, r["gin"], own_sem.at[7])

    @pl.when(place.s == 0)
    def _():
        token_load.start()

    @pl.when(place.s == 3)
    def _():
        cot_load.start()

    mine = lax.broadcasted_iota(jnp.int32, (1, 128), 1) // 32 == place.d % 4

    def spot(x):
        x = x.astype(F32)
        return jnp.where(mine, jnp.concatenate([x, x, x, x], axis=1), 0.0)

    small[place.d, 0:3] = spot(gains[...])
    small[place.d, 3:10] = spot(vecs[...])
    small[place.d, 10:11] = mgain[...].astype(F32)
    small[place.d, 11:13] = mbias[...].astype(F32)
    small[place.d, 13:16] = jnp.zeros((3, 128), F32)
    place.barrier()

    def own(k):
        if k == 3:
            w[place.d, UP : UP + 8] = own_up[...].T.reshape(8, 16, WIDTH)
        for copy in {1: loads[4:5], 2: loads[5:6], 4: loads[2:4], 5: loads[:2]}.get(k, ()):
            copy.wait()

    def forward_copy(n):
        cols = pl.ds(n * 256, 256)
        return remote(
            out.at[:, cols], r["zin"].at[:, cols], xsend.at[n], xrecv.at[n], (place.s + 1) % 4, place.d
        )

    def send_forward(n):
        @pl.when(place.s < 3)
        def _():
            forward_copy(n).start()

    gather = Gather(place, w, small, sib, gsend, grecv, hsend, hrecv)

    def setup():
        for q in range(8):
            r["pd"][:, q * 128 : (q + 1) * 128] = small[4 * q] + small[4 * q + 1] + small[4 * q + 2] + small[4 * q + 3]
        for q in range(32):
            r["pm"][:, q * 128 : (q + 1) * 128] = small[q]
        r["pq"][:, :WIDTH] = r["pd"][4:5, :]
        r["pq"][:, WIDTH : 2 * WIDTH] = jnp.zeros((1, WIDTH), F32)
        r["pq"][:, 2 * WIDTH :] = r["pd"][5:6, :]
        heads = jnp.concatenate([hscale[...].astype(F32), jnp.zeros((1, 112), F32)], axis=1)
        r["hs"][...] = lax.dot_general(
            jnp.broadcast_to(heads, (8, 128)), head_columns(), (((1,), (0,)), ((), ())),
            precision=lax.Precision.HIGHEST, preferred_element_type=F32,
        )
        row = lax.broadcasted_iota(jnp.int32, (TOK, TOK), 0)
        col = lax.broadcasted_iota(jnp.int32, (TOK, TOK), 1)
        seg_key = jnp.broadcast_to(seg[...].astype(F32), (TOK, TOK))
        ok = (seg_key == seg_key.T) & (col <= row) & (row // 64 == col // 64)
        r["ok"][...] = jnp.where(ok, 1.0, 0.0)

    begins = place.s == 0

    def ready(k):
        work = gather.work
        if k == 0:
            setup()

            @pl.when(begins)
            def _():
                token_load.wait()
                layer.first_norm()
        elif k == 1:
            for c in range(2):
                work.add(lambda c=c: layer.qkv(2 * c, 2), begins)
            for c in range(4):
                work.add(lambda c=c: layer.attention(2 * c, 2), begins)
        elif k == 2:
            work.add(layer.project, begins)
            work.add(layer.middle_norms, begins)
        elif k == 3:
            for c in range(2):
                work.add(lambda c=c: layer.up(2 * c, 2), begins)
            for c in range(2):
                work.add(lambda c=c: layer.inner_norm(4 * c, 4), begins)

    gather.run(own, ready)

    @pl.when(begins)
    def _():
        layer.down(send_forward)

    @pl.when(place.s == 3)
    def _():
        cot_load.wait()

        @each(4)
        def _(i):
            at = rows_of(i, 32)
            row = lax.broadcasted_iota(jnp.int32, (32, WIDTH), 0) + 32 * i
            alive = row % 64 < jnp.where(row < 64, live[0], live[1])
            r["gin"][at, :] = jnp.where(alive, r["gin"][at, :].astype(F32), 0.0).astype(BF16)

    @pl.when(place.s > 0)
    def _():
        for n in range(4):
            forward_copy(n).wait_recv()
        layer.first_norm()
        layer.qkv()
        layer.attention()
        layer.project()
        layer.middle_norms()
        layer.up()
        layer.inner_norm()
        layer.down(send_forward)

    layer.prepare()
    gather.close()
    pl.semaphore_signal(sib_ok, inc=1, device_id=(place.s, place.sib), device_id_type=MESH)

    @pl.when(place.s < 3)
    def _():
        for n in range(4):
            forward_copy(n).wait_send()

    def backward_copy(i):
        at = pl.ds(i * 32, 32)
        return remote(gz.at[at], r["gin"].at[at], bsend.at[i], brecv.at[i], (place.s + 3) % 4, place.d)

    def send_backward(i):
        @pl.when(place.s > 0)
        def _():
            backward_copy(i).start()

    @pl.when(place.s < 3)
    def _():
        for i in range(4):
            backward_copy(i).wait_recv()

    @pl.when(place.s > 0)
    def _():
        layer.back_down(0, 1, 2, 3)
        layer.back_inner()
        layer.back_up()
        layer.back_middle()
        layer.back_project()
        layer.back_attention()
        layer.back_qkv()
        layer.back_first(send_backward)

    def first_section(*phases):
        @pl.when(place.s == 0)
        def _():
            for phase in phases:
                phase()

    scatter = Scatter(place, w, small, sib, ssib, land, sland, back, ssend, srecv, hsend, hrecv)
    n = len(SCATTER_STEPS)

    def stage(step, t):
        for k in SCATTER_STEPS[t] if 0 <= t < n else ():
            if k == AWAY:
                pl.when(place.s > 0)(lambda k=k: step(k))
            else:
                step(k)
        scatter.work.pop()

    def flow(t):
        for late, step in enumerate((scatter.halves, scatter.wholes, scatter.far)):
            for j in (3, 1, 2, 0):
                stage(lambda k, j=j, step=step: step(k, j), t - 1 - late)
        stage(scatter.near, t - 4)
        stage(lambda k: scatter.last(k, total, small_total), t - 5)

    work = scatter.work
    halfs = (slice(0, 512), slice(512, 1024))
    for c in range(2):
        work.add(lambda c=c: layer.back_inner(4 * c, 4), begins)
    for half in halfs:
        work.add(lambda half=half: layer.back_up(half), begins)
    for c in range(4):
        work.add(lambda c=c: layer.grad_up(2 * c, 2))
    work.add(lambda: scatter.to_sibling(1))
    work.add(lambda: scatter.to_sibling(2), tag="up")
    work.add(layer.back_middle, begins)
    work.add(layer.back_project, begins)
    for c in range(4):
        work.add(lambda c=c: layer.back_attention(2 * c, 2), begins)
    for half in halfs:
        work.add(lambda half=half: layer.back_qkv(half), begins)
    work.add(lambda: layer.back_first(send_backward), begins)
    for c in range(4):
        work.add(lambda c=c: layer.grad_in(2 * c, 2))
    for c in range(2):
        work.add(lambda c=c: layer.grad_out(c))
    work.add(lambda: scatter.to_sibling(3))
    work.add(lambda: scatter.to_sibling(5), tag="in")
    work.add(layer.inner_sums)
    work.add(layer.other_sums)
    work.add(lambda: layer.grad_small(small))
    work.add(lambda: scatter.to_sibling(4), tag="small")

    first_section(lambda: layer.back_down(2, 3))
    layer.grad_down(2, 3)
    pl.semaphore_wait(sib_ok, 1)
    scatter.to_sibling(0)
    first_section(lambda: layer.back_down(0, 1))
    layer.grad_down(0, 1)
    scatter.to_sibling(AWAY)
    flow(1)

    @pl.when(begins)
    def _():
        pl.semaphore_wait(lent_ok, 1)
        scatter.lend()

    work.until("up")
    flow(2)
    flow(3)

    @pl.when(place.s == 3)
    def _():
        pl.semaphore_signal(lent_ok, inc=1, device_id=(0, place.d), device_id_type=MESH)

    work.until("in")
    flow(4)
    work.until("small")
    for t in range(5, n + 5):
        flow(t)
    pl.when(place.s == 3)(scatter.aid)

    @pl.when(place.s == 0)
    def _():
        scatter.returned().wait_recv()
        u, count = LENT
        total[u : u + count] = back[...].astype(F32)

    scatter.close()

    @pl.when(place.s > 0)
    def _():
        for i in range(4):
            backward_copy(i).wait_send()


VSPEC = pl.BlockSpec(memory_space=pltpu.VMEM)
ASPEC = pl.BlockSpec(memory_space=pl.ANY)
SSPEC = pl.BlockSpec(memory_space=pltpu.SMEM)
DMA = pltpu.SemaphoreType.DMA


def run_layers(*args):
    g, s = (len(GATHER) + 1, 16), (len(SCATTER) + 1, 12)
    return pl.pallas_call(
        kernel,
        out_shape=[
            jax.ShapeDtypeStruct((TOK, WIDTH), BF16),
            jax.ShapeDtypeStruct((TOK, WIDTH), BF16),
            jax.ShapeDtypeStruct((UNITS, 16, WIDTH), F32),
            jax.ShapeDtypeStruct((16, 128), F32),
        ],
        in_specs=[ASPEC, ASPEC, SSPEC, VSPEC, ASPEC, ASPEC, VSPEC, ASPEC, VSPEC, VSPEC, VSPEC, VSPEC, VSPEC],
        out_specs=[VSPEC] * 4,
        scratch_shapes=[
            pltpu.VMEM((32, UNITS, 16, WIDTH), BF16),
            pltpu.VMEM((32, 16, 128), F32),
            pltpu.VMEM((16, UNITS, 16, WIDTH), BF16),
            pltpu.VMEM((16, 16, 128), F32),
        ]
        + [pltpu.VMEM((SHARE, slots, units, 16, WIDTH), BF16) for slots, units in LANDING]
        + [pltpu.VMEM((slots, 4 * units, 128), F32) for slots, units in LANDING]
        + [pltpu.VMEM((LENT[1], 16, WIDTH), BF16)]
        + [pltpu.VMEM(*v) for v in HELD.values()]
        + [DMA(g[:1]), DMA(g), DMA((8,)), DMA((4,)), DMA((4,)), DMA((4,)), DMA((4,)), DMA(s[:1]), DMA(s), DMA((4,)), DMA((9,))]
        + [pltpu.SemaphoreType.REGULAR] * 2,
        compiler_params=pltpu.CompilerParams(collective_id=1, has_side_effects=True, vmem_limit_bytes=VMEM_LIMIT),
        name="layers",
    )(*args)


def finish_kernel(out, gz, total, small, out2, gz2, g_in, g_out, g_up, g_down, g_gains, g_vecs, g_mgain, g_mbias, g_heads):
    out2[...] = out[...]
    gz2[...] = gz[...]
    g_in[...] = total[IN : IN + 6]
    g_out[...] = total[OUT : OUT + 2]
    for q in range(4):
        g_down[:, :, q * 1024 : (q + 1) * 1024] = total[DOWN + 2 * q : DOWN + 2 * q + 2]
    g_up[...] = total[UP : UP + 8].reshape(128, WIDTH).T
    lane = lax.axis_index("dp") % 4
    thin = jnp.zeros((10, 32), F32)
    for j in range(4):
        thin = jnp.where(lane == j, small[0:10, 32 * j : 32 * (j + 1)], thin)
    for i in range(3):
        g_gains[i] = thin[i : i + 1]
    for i in range(7):
        g_vecs[i] = thin[3 + i : 4 + i]
    g_mgain[...] = small[10:11, :]
    g_mbias[...] = small[11:13, :]
    g_heads[...] = small[13:14, :16]


def finish(*args):
    f = jax.ShapeDtypeStruct
    return pl.pallas_call(
        finish_kernel,
        out_shape=[
            f((TOK, WIDTH), BF16), f((TOK, WIDTH), BF16), f((6, 16, WIDTH), F32), f((2, 16, WIDTH), F32),
            f((WIDTH, 128), F32), f((2, 16, FF), F32), f((3, 1, 32), F32), f((7, 1, 32), F32), f((1, 128), F32),
            f((2, 128), F32), f((1, 16), F32),
        ],
        in_specs=[VSPEC] * 4,
        out_specs=[VSPEC] * 11,
        name="finish",
    )(*args)


def body(
    tokens, cotangent, live_counts, segments, attn_input, attn_output, feed_up, feed_down,
    norm_gains, vector_bias, mid_gain, mid_bias, head_scale,
):
    res = run_layers(
        tokens, cotangent, live_counts, segments[None, :], attn_input[0].T.reshape(6, 16, WIDTH),
        attn_output[0].T.reshape(2, 16, WIDTH), feed_up[0], feed_down[0].T.reshape(2, 16, FF), norm_gains[0],
        vector_bias[0], mid_gain, mid_bias[0], head_scale,
    )
    out, gz, g_in, g_out, g_up, g_down, g_gains, g_vecs, g_mgain, g_mbias, g_heads = finish(*res)
    return (
        out[None],
        gz[None],
        g_in.reshape(96, WIDTH).T[None],
        g_out.reshape(32, WIDTH).T[None],
        g_up[None],
        g_down.reshape(32, FF).T[None],
        g_gains.transpose(1, 0, 2),
        g_vecs.transpose(1, 0, 2),
        g_mgain,
        g_mbias[None],
        g_heads,
    )


def solution(mesh):
    return jax.shard_map(
        body,
        mesh=mesh,
        in_specs=(
            P("dp", None), P("dp", None), P("dp"), P("dp"),
            P("pipe", None, "dp"), P("pipe", None, "dp"), P("pipe", None, "dp"), P("pipe", None, "dp"),
            P("pipe", None, "dp"), P("pipe", None, "dp"), P("pipe", "dp"), P("pipe", None, "dp"), P("pipe", None),
        ),
        out_specs=(
            P("pipe", "dp", None), P("pipe", "dp", None),
            P("pipe", None, "dp"), P("pipe", None, "dp"), P("pipe", None, "dp"), P("pipe", None, "dp"),
            P("pipe", None, "dp"), P("pipe", None, "dp"), P("pipe", "dp"), P("pipe", None, "dp"), P("pipe", None),
        ),
        check_vma=False,
    )
```

profile of v0, /device:TPU:0, one launch (start us, length us, event | category | flops | bytes accessed | tf_op | source)
XLA Modules:
  0.0 264.3 jit_solution(5490673667792723010)
XLA Ops:
  0.6 260.4 %layers.1 = (bf16[128,1024]{1,0:T(8,128)(2,1)}, bf16[128,1024]{1,0:T(8,128)(2,1)}, f32[24,16,1024]{2,1,0:T(8,128)}, f32[16,128]{1,0:T(8,128)}) custom-call(bf16[128,1024]{1,0:T(8,128)(2,1)} %refs_0_.1, bf16[128,1024]{1,0:T(8,128)(2,1)} %refs_1_.1, s32[2]{0:T(128)} %refs_2_.1, s32[1,128]{1,0:T(1,128)} %bitcast.47, bf16[6,16,1024]{2,1,0:T(8,128)(2,1)} %bitcast.43, ...), custom_call_target="tpu_custom_call" | custom-call | tf_op jit(solution)/shard_map/layers/pallas_call | solution.py:1096
  261.0 3.2 %finish.1 = (bf16[128,1024]{1,0:T(8,128)(2,1)}, bf16[128,1024]{1,0:T(8,128)(2,1)}, f32[6,16,1024]{2,1,0:T(8,128)}, f32[2,16,1024]{2,1,0:T(8,128)}, f32[1024,128]...) custom-call(bf16[128,1024]{1,0:T(8,128)(2,1)} %get-tuple-element.26., ...), custom_call_target="tpu_custom_call" | custom-call | tf_op jit(solution)/shard_map/finish/pallas_call | solution.py:1146
where the time goes:
time: 264 us
  Pallas kernels  264 us (100%)
    pallas_call x1, Pallas kernels, run_layers(): pl.pallas_call(kernel, out_shape=[jax.ShapeDtypeStruct((TOK, WIDTH), BF16...  260 us

commit v1 on v0

--- a/solution.py
+++ b/solution.py
@@ -438,7 +438,7 @@
     def inner_norm(self, first=0, count=8):
         r, pm = self.r, self.r["pm"]
 
-        @each(count, 2)
+        @each(count, 2 if count == 8 else 1)
         def _(i):
             i = i + first
             at = rows_of(i, 16)
@@ -479,7 +479,7 @@
     def back_inner(self, first=0, count=8):
         r, pm = self.r, self.r["pm"]
 
-        @each(count, 2)
+        @each(count, 2 if count == 8 else 1)
         def _(i):
             i = i + first
             at = rows_of(i, 16)
@@ -698,10 +698,10 @@
 
         @each(dst.shape[0])
         def _(u):
-            acc = dst[u].astype(F32)
+            acc = dst[u].astype(out.dtype)
             for src in srcs:
-                acc = acc + src[u].astype(F32)
-            out[u] = acc.astype(out.dtype)
+                acc = acc + src[u].astype(out.dtype)
+            out[u] = acc
 
     def halves(self, k, j):
         p = self.p
@@ -1020,8 +1020,8 @@
         work.add(lambda c=c: layer.back_inner(4 * c, 4), begins)
     for half in halfs:
         work.add(lambda half=half: layer.back_up(half), begins)
-    for c in range(4):
-        work.add(lambda c=c: layer.grad_up(2 * c, 2))
+    for c in range(8):
+        work.add(lambda c=c: layer.grad_up(c, 1))
     work.add(lambda: scatter.to_sibling(1))
     work.add(lambda: scatter.to_sibling(2), tag="up")
     work.add(layer.back_middle, begins)
@@ -1031,8 +1031,8 @@
     for half in halfs:
         work.add(lambda half=half: layer.back_qkv(half), begins)
     work.add(lambda: layer.back_first(send_backward), begins)
-    for c in range(4):
-        work.add(lambda c=c: layer.grad_in(2 * c, 2))
+    for c in range(8):
+        work.add(lambda c=c: layer.grad_in(c, 1))
     for c in range(2):
         work.add(lambda c=c: layer.grad_out(c))
     work.add(lambda: scatter.to_sibling(3))

time: 264 us -> 261 us (0.989)
  Pallas kernels: 264 us -> 259 us
    pallas_call x1, Pallas kernels: 260 us -> 256 us  [run_layers(): pl.pallas_call(kernel, out_shape=[jax.ShapeDtypeStruct((TOK, WIDTH), BF16...]
where the time goes in v1:
time: 261 us; the launch traced here: 260 us
  Pallas kernels  259 us (99%)
    pallas_call x1, Pallas kernels, run_layers(): pl.pallas_call(kernel, out_shape=[jax.ShapeDtypeStruct((TOK, WIDTH), BF16...  256 us

profile of v1, /device:TPU:0, one launch (start us, length us, event | category | flops | bytes accessed | tf_op | source)
XLA Modules:
  0.0 260.1 jit_solution(18338835027580170353)
XLA Ops:
  0.6 256.1 %layers.1 = (bf16[128,1024]{1,0:T(8,128)(2,1)}, bf16[128,1024]{1,0:T(8,128)(2,1)}, f32[24,16,1024]{2,1,0:T(8,128)}, f32[16,128]{1,0:T(8,128)}) custom-call(bf16[128,1024]{1,0:T(8,128)(2,1)} %refs_0_.1, bf16[128,1024]{1,0:T(8,128)(2,1)} %refs_1_.1, s32[2]{0:T(128)} %refs_2_.1, s32[1,128]{1,0:T(1,128)} %bitcast.47, bf16[6,16,1024]{2,1,0:T(8,128)(2,1)} %bitcast.43, ...), custom_call_target="tpu_custom_call" | custom-call | tf_op jit(solution)/shard_map/layers/pallas_call | solution.py:1096
  256.8 3.2 %finish.1 = (bf16[128,1024]{1,0:T(8,128)(2,1)}, bf16[128,1024]{1,0:T(8,128)(2,1)}, f32[6,16,1024]{2,1,0:T(8,128)}, f32[2,16,1024]{2,1,0:T(8,128)}, f32[1024,128]...) custom-call(bf16[128,1024]{1,0:T(8,128)(2,1)} %get-tuple-element.26., ...), custom_call_target="tpu_custom_call" | custom-call | tf_op jit(solution)/shard_map/finish/pallas_call | solution.py:1146

commit v2 on v1

--- a/solution.py
+++ b/solution.py
@@ -268,18 +268,18 @@
                 begun += 1
             stage(self.ring, t)
             self.work.pop()
+            count = 1 if t <= n else 0
             stage(self.far, t - 1)
-            self.work.pop()
+            self.work.pop(count)
             for j in range(4):
                 stage(lambda k, j=j: self.second(k, j), t - 2)
-                self.work.pop()
+                self.work.pop(count)
             for j in range(4):
                 stage(lambda k, j=j: self.last(k, j), t - 3)
-                self.work.pop()
+                self.work.pop(count)
             if 4 <= t < 8:
                 pl.when(s == 0)(lambda t=t: self.relay(t - 4))
-
-            self.work.pop()
+            self.work.pop(1 if count else 8)
             if t >= 3:
                 self.whole(t - 3)
                 ready(t - 3)

time: 261 us -> 258 us (0.989)
  no operation moved by 1% of the time
where the time goes in v2:
time: 258 us
  Pallas kernels  257 us (100%)
    pallas_call x1, Pallas kernels, run_layers(): pl.pallas_call(kernel, out_shape=[jax.ShapeDtypeStruct((TOK, WIDTH), BF16...  254 us

profile of v2, /device:TPU:0, one launch (start us, length us, event | category | flops | bytes accessed | tf_op | source)
XLA Modules:
  0.0 258.2 jit_solution(4317909225146637943)
XLA Ops:
  0.6 254.2 %layers.1 = (bf16[128,1024]{1,0:T(8,128)(2,1)}, bf16[128,1024]{1,0:T(8,128)(2,1)}, f32[24,16,1024]{2,1,0:T(8,128)}, f32[16,128]{1,0:T(8,128)}) custom-call(bf16[128,1024]{1,0:T(8,128)(2,1)} %refs_0_.1, bf16[128,1024]{1,0:T(8,128)(2,1)} %refs_1_.1, s32[2]{0:T(128)} %refs_2_.1, s32[1,128]{1,0:T(1,128)} %bitcast.47, bf16[6,16,1024]{2,1,0:T(8,128)(2,1)} %bitcast.43, ...), custom_call_target="tpu_custom_call" | custom-call | tf_op jit(solution)/shard_map/layers/pallas_call | solution.py:1096
  254.9 3.2 %finish.1 = (bf16[128,1024]{1,0:T(8,128)(2,1)}, bf16[128,1024]{1,0:T(8,128)(2,1)}, f32[6,16,1024]{2,1,0:T(8,128)}, f32[2,16,1024]{2,1,0:T(8,128)}, f32[1024,128]...) custom-call(bf16[128,1024]{1,0:T(8,128)(2,1)} %get-tuple-element.26., ...), custom_call_target="tpu_custom_call" | custom-call | tf_op jit(solution)/shard_map/finish/pallas_call | solution.py:1146
